TPU v7x, 256 devices: a whole 4x4x8 slice. The times are simulated.
256 devices in a mesh: outer: 16 (over y, x), inner: 16 (over z, core).
Axes of the slice: x: 4, y: 4, z: 8, core: 2. Of those that a mesh axis runs over, the one named last changes fastest.
Arguments:
- tokens: bfloat16 [98304, 1024], P(('outer', 'inner')), may hold values from -6 to 6
- log_decay: float32 [98304, 16], P(('outer', 'inner')), may hold values from -1 to 0, as said below
- query_weight: bfloat16 [1024, 1024], replicated, may hold values from -0.1875 to 0.1875
- key_weight: bfloat16 [1024, 1024], replicated, may hold values from -0.1875 to 0.1875
- value_weight: bfloat16 [1024, 1024], replicated, may hold values from -0.1875 to 0.1875
- norm_gain: float32 [1024], replicated, may hold values from 0.1 to 1.9
- output_weight: bfloat16 [1024, 1024], replicated, may hold values from -0.1875 to 0.1875
Outputs:
- mixed: bfloat16 [98304, 1024], P(('outer', 'inner'))
Inputs may be any that keep to these rules, and one draw needn't show every extreme that they name: log_decay is negative.
All inputs are finite; a program needn't handle non-finite values.
Results may differ from a plain program's by a relative error of at most 0.0063.
Values sent between devices are 32-bit elements; how exact they have to be, the bound alone decides.
A program may use at most 320 MiB of HBM per device.

v0:
```python
import jax
import jax.numpy as jnp
from jax import lax
from jax.sharding import PartitionSpec as P


def prefix(value, axis, join, neutral):
    count, mine = (lax.axis_size(axis), lax.axis_index(axis))
    pieces = jax.tree.map(lambda part: lax.all_gather(part, axis), value)
    running = jax.tree.map(
        lambda part, zero: jnp.full_like(part, 0) + jnp.asarray(zero, part.dtype), value, neutral
    )

    def lap(position, running):
        longer = join(running, jax.tree.map(lambda part: part[position], pieces))
        return jax.tree.map(lambda new, old: jnp.where(position < mine, new, old), longer, running)

    return lax.fori_loop(0, count - 1, lap, running)


def broadcast(value, axis, source):
    kept = jnp.where(lax.axis_index(axis) == source, value, 0).astype(value.dtype)
    return lax.psum(kept, axis)


def local_head(q_head, k_head, v_head, g_head):
    cum = jnp.cumsum(g_head)
    count = cum.shape[0]
    rows = lax.broadcasted_iota(jnp.int32, (count, count), 0)
    cols = lax.broadcasted_iota(jnp.int32, (count, count), 1)
    lower = cols <= rows
    diff = jnp.where(lower, cum[:, None] - cum[None, :], 0.0)
    decay = jnp.where(lower, jnp.exp(diff), 0.0)
    scores = jnp.dot(q_head, k_head.T, preferred_element_type=jnp.float32)
    weights = (scores * decay).astype(jnp.bfloat16)
    intra = jnp.dot(weights, v_head, preferred_element_type=jnp.float32)
    last = cum[-1]
    scaled = (k_head.astype(jnp.float32) * jnp.exp(last - cum)[:, None]).astype(jnp.bfloat16)
    local = jnp.dot(scaled.T, v_head, preferred_element_type=jnp.float32)
    return (intra, local, jnp.exp(last))


def combine(earlier, later):
    return (earlier[0] * later[0], later[0][:, None, None] * earlier[1] + later[1])


def shards(tokens, log_decay, query_weight, key_weight, value_weight, norm_gain, output_weight):
    count = tokens.shape[0]
    heads = log_decay.shape[1]
    queries = jax.nn.silu(jnp.dot(tokens, query_weight, preferred_element_type=jnp.float32)).astype(
        jnp.bfloat16
    )
    keys = jax.nn.silu(jnp.dot(tokens, key_weight, preferred_element_type=jnp.float32)).astype(
        jnp.bfloat16
    )
    value_rows = jnp.dot(tokens, value_weight, preferred_element_type=jnp.float32).astype(
        jnp.bfloat16
    )
    split = lambda arr: arr.reshape(count, heads, -1).transpose(1, 0, 2)
    queries, keys, value_rows = (split(queries), split(keys), split(value_rows))
    intra, local, fall = lax.map(
        lambda token_parts: local_head(*token_parts), (queries, keys, value_rows, log_decay.T)
    )
    own = (fall, local)
    identity = (jnp.ones_like(fall), jnp.zeros_like(local))
    inner_before = prefix(own, "inner", combine, identity)
    inclusive = combine(inner_before, own)
    total = (
        broadcast(inclusive[0], "inner", lax.axis_size("inner") - 1),
        broadcast(inclusive[1], "inner", lax.axis_size("inner") - 1),
    )
    outer_before = prefix(total, "outer", combine, identity)
    incoming = combine(outer_before, inner_before)[1]
    cum = jnp.cumsum(log_decay, axis=0)
    qfloat = queries.astype(jnp.float32)
    inter = (
        jnp.einsum("htd,hde->the", qfloat, incoming, precision=lax.Precision.HIGHEST)
        * jnp.exp(cum)[:, :, None]
    )
    attended = intra.transpose(1, 0, 2) + inter
    scale = lax.rsqrt(jnp.mean(attended * attended, axis=-1, keepdims=True) + 1e-05)
    normalized_output = ((attended * scale).reshape(count, -1) * norm_gain).astype(jnp.bfloat16)
    return jnp.dot(normalized_output, output_weight, preferred_element_type=jnp.float32).astype(
        jnp.bfloat16
    )


def solution(mesh):
    in_specs = (P(("outer", "inner"), None), P(("outer", "inner"), None), P(), P(), P(), P(), P())
    out_specs = P(("outer", "inner"), None)
    return jax.shard_map(shards, mesh=mesh, in_specs=in_specs, out_specs=out_specs, check_vma=False)
```

profile of v0, /device:TPU:1, one launch (start us, length us, event | category | flops | bytes accessed | tf_op | source)
XLA Modules:
  0.0 440.0 jit_solution(5234878555848884277)
XLA Ops:
  8.1 3.2 multiply_convert_fusion.2
  12.8 3.9 multiply_convert_fusion.1
  16.6 2.3 copy.24
  18.9 3.7 convolution_convert_fusion.1
  22.6 2.3 copy.25
  25.0 115.7 %while.47 = (s32[]{:T(128)}, f32[16,384,64]{1,2,0:T(8,128)}, f32[16,64,64]{2,1,0:T(8,128)}, f32[16]{0:T(128)S(1)}, bf16[16,384,64]{1,2,0:T(8,128)(2,1)S(1)}, /*i...) while((s32[]{:T(128)}, f32[16,384,64]{1,2,0:T(8,128)}, ...), condition=%wide.region_3.4_spmd.clone, body=%wide.region_0.3_spmd.sunk.clone | while | flops 41902472 | bytes 594653 | solution.py:61
  27.8 1.7 fusion.75
  29.5 1.9 fusion.74
  35.0 1.7 fusion.75
  36.7 1.9 fusion.74
  42.2 1.7 fusion.75
  43.9 1.9 fusion.74
  49.5 1.7 fusion.75
  51.2 1.9 fusion.74
  56.7 1.7 fusion.75
  58.4 1.9 fusion.74
  63.9 1.7 fusion.75
  65.6 1.9 fusion.74
  71.2 1.7 fusion.75
  72.9 1.9 fusion.74
  80.1 1.9 fusion.74
  85.6 1.7 fusion.75
  87.3 1.9 fusion.74
  92.9 1.7 fusion.75
  94.5 1.9 fusion.74
  100.1 1.7 fusion.75
  101.8 1.9 fusion.74
  107.3 1.7 fusion.75
  109.0 1.9 fusion.74
  114.5 1.7 fusion.75
  116.2 1.9 fusion.74
  121.8 1.7 fusion.75
  123.5 1.9 fusion.74
  129.0 1.7 fusion.75
  130.7 1.9 fusion.74
  136.2 1.7 fusion.75
  137.9 1.9 fusion.74
  142.2 28.4 %all-reduce = f32[256]{0:T(256)S(1)} all-reduce(f32[256]{0:T(256)S(1)} %dynamic-update-slice), channel_id=2, replica_groups=mesh['outer'=16,'inner'=16] {'inner'}, use_global_device_ids=true, to_apply=%add | all-reduce | flops 256 | bytes 2048
  170.7 30.5 %all-gather.8.cloned.1.call-done = f32[256,64,64]{2,1,0:T(8,128)} async-done(((f32[16,64,64]{2,1,0:T(8,128)}), f32[256,64,64]{2,1,0:T(8,128)}) %all-gather.8.cloned.1.call-update) | async-done | bytes 4194320 | tf_op jit(solution)/shard_map/all_gather | solution.py:9
  201.2 18.3 %while.48 = (s32[]{:T(128)}, f32[16]{0:T(128)S(1)}, f32[16,64,64]{2,1,0:T(8,128)S(1)}, s32[]{:T(128)}, f32[16,16]{1,0:T(8,128)S(1)}, /*index=5*/f32[16,16,64,64]{3,2,1,0:T(8,128)}) while((s32[]{:T(128)}, f32[16]{0:T(128)S(1)}, f32[16,64,64]{2,1,0:T(8,128)S(1)}, s32[]{:T(128)}, f32[16,16]{1,0:T(8,128)S(1)}, ...), condition=%wide.region_5.6_spmd.clone.clone, body=%wide.region_4.5_spmd.clone.sunk.clone | while | flops 262196 | bytes 786851 | solution.py:18
  219.5 2.0 select_bitcast_fusion
  221.5 107.8 %all-reduce.3.cloned.1.call-done = f32[1,16,64,64]{3,2,1,0:T(8,128)} async-done(((f32[1,16,64,64]{3,2,1,0:T(8,128)}), f32[1,16,64,64]{3,2,1,0:T(8,128)}) %all-reduce.3.cloned.1.call-update) | async-done | bytes 262160 | tf_op jit(solution)/shard_map/psum | solution.py:23
  330.5 23.6 %psum.14 = f32[1,16]{1,0:T(1,128)S(1)} all-reduce(f32[1,16]{1,0:T(1,128)S(1)} %fusion.37), channel_id=1, replica_groups=mesh['outer'=16,'inner'=16] {'inner'}, use_global_device_ids=true, to_apply=%region_6.7 | all-reduce | flops 16 | bytes 128 | tf_op jit(solution)/shard_map/psum | solution.py:23
  354.1 16.7 %all-gather.2 = f32[16,1,16]{2,1,0:T(1,128)S(1)} all-gather(f32[1,1,16]{2,1,0:T(1,128)S(1)} %bitcast.147), channel_id=1, replica_groups=mesh['outer'=16,'inner'=16] {'outer'}, dimensions={0}, use_global_device_ids=true | all-gather | bytes 1088 | tf_op jit(solution)/shard_map/all_gather | solution.py:9
  370.9 37.3 %all-gather.6.cloned.1.call-done = f32[16,16,64,64]{3,2,1,0:T(8,128)} async-done(((f32[1,16,64,64]{3,2,1,0:T(8,128)}), f32[16,16,64,64]{3,2,1,0:T(8,128)}) %all-gather.6.cloned.1.call-update) | async-done | bytes 4194320 | tf_op jit(solution)/shard_map/all_gather | solution.py:9
  408.2 18.2 %while.49 = (s32[]{:T(128)}, f32[16,64,64]{2,1,0:T(8,128)S(1)}, s32[]{:T(128)}, f32[16,16]{1,0:T(8,128)S(1)}, f32[16,16,64,64]{3,2,1,0:T(8,128)}) while((s32[]{:T(128)}, f32[16,64,64]{2,1,0:T(8,128)S(1)}, s32[]{:T(128)}, f32[16,16]{1,0:T(8,128)S(1)}, f32[16,16,64,64]{3,2,1,0:T(8,128)}) %tuple.108), condition=%wide.region_9.10_spmd.clone.clone, body=%wide.region_8.9_spmd.clone.sunk.clone | while | flops 262148 | bytes 786713 | solution.py:18
  426.4 2.9 multiply_reduce_fusion
  431.5 1.9 convolution_convert_fusion
  (275 shorter events, 91.7 us)
Async XLA Ops:
  6.5 1.6 copy-start
  6.5 194.6 %all-gather.8.cloned.1.call-start = ((), (), s32[]{:S(2)}) async-start(), calls=%async_computation.2 | async-start | bytes 8912896 | tf_op jit(solution)/shard_map/all_gather | solution.py:9
  22.6 2.3 copy-start.3
  25.0 115.8 %copy-start.5 = (u32[256]{0:T(256)S(1)}, u32[256]{0:T(256)}, u32[]{:S(2)}) copy-start(u32[256]{0:T(256)} %constant.98) | copy-start | bytes 3076
  140.6 80.8 %copy-start.1 = (bf16[16,384,64]{1,2,0:T(8,128)(2,1)}, bf16[16,384,64]{1,2,0:T(8,128)(2,1)S(1)}, u32[]{:S(2)}) copy-start(bf16[16,384,64]{1,2,0:T(8,128)(2,1)S(1)} %get-tuple-element.586) | copy-start | bytes 2359300
  140.7 188.6 %all-reduce.3.cloned.1.call-start = ((), (), s32[]{:S(2)}) async-start(), calls=%async_computation | async-start | bytes 1048576 | tf_op jit(solution)/shard_map/psum | solution.py:23
  221.5 186.7 %all-gather.6.cloned.1.call-start = ((), (), s32[]{:S(2)}) async-start(), calls=%async_computation.1 | async-start | bytes 8912896 | tf_op jit(solution)/shard_map/all_gather | solution.py:9
  429.3 0.7 copy-start.4
  430.0 1.6 copy-start.2
Sparse Core Ops, SparseCore 0:
  140.8 60.3 all-gather.7
  221.6 107.6 all-reduce.2
  332.0 76.1 all-gather.5
where the time goes:
time: 445 us; the launch traced here: 440 us
  waiting for transfers between devices  176 us (40%)
  matrix products  73.1 us (16%)
  blocking collectives  68.7 us (15%)
  other arithmetic  55.9 us (13%)
  local copies, waits for them, and re-layouts  40.5 us (9%)
  between operations  13.8 us (3%)
  loops' own time  12.1 us (3%)
    psum x1, waiting for transfers between devices, broadcast(): return lax.psum(kept, axis)  108 us
    all_gather x2, waiting for transfers between devices, prefix(): pieces = jax.tree.map(lambda part: lax.all_gather(part, axis), value)  67.8 us
    select_n x45, other arithmetic, lap(): jnp.where(position < mine, new, old)  35.5 us
    dot_general x16, matrix products, local_head(): intra = jnp.dot(weights, v_head, preferred_element_type=jnp.float32)  30.6 us
    unnamed x1, blocking collectives  28.4 us
    dot_general x16, matrix products, local_head(): local = jnp.dot(scaled.T, v_head, preferred_element_type=jnp.float32)  27 us
    psum x1, blocking collectives, broadcast(): return lax.psum(kept, axis)  23.6 us
    all_gather x1, blocking collectives, prefix(): pieces = jax.tree.map(lambda part: lax.all_gather(part, axis), value)  16.7 us
  transfers between devices with their start and end apart: 3, of which 3 were waited for; matrix products, arithmetic and copies ran while one was open for 0% of the time, Pallas kernels for 0%

commit v1 on v0

--- a/solution.py
+++ b/solution.py
@@ -2,6 +2,7 @@
 import jax.numpy as jnp
 from jax import lax
 from jax.sharding import PartitionSpec as P
+from jax.lax import all_gather
 
 
 def prefix(value, axis, join, neutral):
@@ -20,7 +21,7 @@
 
 def broadcast(value, axis, source):
     kept = jnp.where(lax.axis_index(axis) == source, value, 0).astype(value.dtype)
-    return lax.psum(kept, axis)
+    return all_gather(kept, axis).sum(axis=0)
 
 
 def local_head(q_head, k_head, v_head, g_head):

time: 445 us -> 393 us (0.88)
  waiting for transfers between devices: 176 us -> 99.2 us
  blocking collectives: 68.7 us -> 85.9 us
  other arithmetic: 55.9 us -> 61.3 us
    psum x1 -> x0, waiting for transfers between devices: 108 us -> none  [broadcast(): return lax.psum(kept, axis)]
    unnamed x1 -> x3, blocking collectives: 28.4 us -> 85.9 us
    all_gather x0 -> x1, waiting for transfers between devices: none -> 54.5 us  [broadcast(): return all_gather(kept, axis).sum(axis=0)]
    psum x1 -> x0, blocking collectives: 23.6 us -> none  [broadcast(): return lax.psum(kept, axis)]
    all_gather x2, waiting for transfers between devices: 67.8 us -> 44.6 us  [prefix(): pieces = jax.tree.map(lambda part: lax.all_gather(part, axis), value)]
    all_gather x1 -> x0, blocking collectives: 16.7 us -> none  [prefix(): pieces = jax.tree.map(lambda part: lax.all_gather(part, axis), value)]
    reduce_sum x0 -> x2, other arithmetic: none -> 5.25 us  [broadcast(): return all_gather(kept, axis).sum(axis=0)]
  transfers between devices with their start and end apart: 3 -> 3, of which waited for: 3 -> 3; matrix products, arithmetic and copies ran while one was open for 0% -> 1% of each run, Pallas kernels for 0% -> 0%
where the time goes in v1:
time: 393 us; the launch traced here: 388 us
  waiting for transfers between devices  99.2 us (25%)
  blocking collectives  85.9 us (22%)
  matrix products  73.1 us (19%)
  other arithmetic  61.3 us (16%)
  local copies, waits for them, and re-layouts  41.5 us (11%)
  between operations  14.5 us (4%)
  loops' own time  12.1 us (3%)
    unnamed x3, blocking collectives  85.9 us
    all_gather x1, waiting for transfers between devices, broadcast(): return all_gather(kept, axis).sum(axis=0)  54.5 us
    all_gather x2, waiting for transfers between devices, prefix(): pieces = jax.tree.map(lambda part: lax.all_gather(part, axis), value)  44.6 us
    select_n x45, other arithmetic, lap(): jnp.where(position < mine, new, old)  35.5 us
    dot_general x16, matrix products, local_head(): intra = jnp.dot(weights, v_head, preferred_element_type=jnp.float32)  30.6 us
    dot_general x16, matrix products, local_head(): local = jnp.dot(scaled.T, v_head, preferred_element_type=jnp.float32)  27 us
    dynamic_slice x48, local copies, waits for them, and re-layouts, shards(): lax.map(lambda token_parts: local_head(*token_parts), (queries, keys, val...  15.3 us
    another operation x1, loops' own time, shards(): lax.map(lambda token_parts: local_head(*token_parts), (queries, keys, val...  11.3 us
  transfers between devices with their start and end apart: 3, of which 3 were waited for; matrix products, arithmetic and copies ran while one was open for 1% of the time, Pallas kernels for 0%

profile of v1, /device:TPU:1, one launch (start us, length us, event | category | flops | bytes accessed | tf_op | source)
XLA Modules:
  0.0 387.7 jit_solution(10563191037203842705)
XLA Ops:
  8.1 3.2 multiply_convert_fusion.2
  12.8 3.9 multiply_convert_fusion.1
  16.6 2.3 copy.33
  18.9 3.7 convolution_convert_fusion.1
  22.6 2.3 copy.34
  25.0 115.7 %while.47 = (s32[]{:T(128)}, f32[16,384,64]{1,2,0:T(8,128)}, f32[16,64,64]{2,1,0:T(8,128)}, f32[16]{0:T(128)S(1)}, bf16[16,384,64]{1,2,0:T(8,128)(2,1)S(1)}, /*i...) while((s32[]{:T(128)}, f32[16,384,64]{1,2,0:T(8,128)}, ...), condition=%wide.region_3.4_spmd.clone, body=%wide.region_0.3_spmd.sunk.clone | while | flops 41902472 | bytes 594653 | solution.py:62
  27.8 1.7 fusion.75
  29.5 1.9 fusion.74
  35.0 1.7 fusion.75
  36.7 1.9 fusion.74
  42.2 1.7 fusion.75
  43.9 1.9 fusion.74
  49.5 1.7 fusion.75
  51.2 1.9 fusion.74
  56.7 1.7 fusion.75
  58.4 1.9 fusion.74
  63.9 1.7 fusion.75
  65.6 1.9 fusion.74
  71.2 1.7 fusion.75
  72.9 1.9 fusion.74
  80.1 1.9 fusion.74
  85.6 1.7 fusion.75
  87.3 1.9 fusion.74
  92.9 1.7 fusion.75
  94.5 1.9 fusion.74
  100.1 1.7 fusion.75
  101.8 1.9 fusion.74
  107.3 1.7 fusion.75
  109.0 1.9 fusion.74
  116.2 1.9 fusion.74
  121.8 1.7 fusion.75
  123.5 1.9 fusion.74
  129.0 1.7 fusion.75
  130.7 1.9 fusion.74
  136.2 1.7 fusion.75
  137.9 1.9 fusion.74
  142.3 28.4 %all-reduce = f32[256]{0:T(256)S(1)} all-reduce(f32[256]{0:T(256)S(1)} %dynamic-update-slice), channel_id=2, replica_groups=mesh['outer'=16,'inner'=16] {'inner'}, use_global_device_ids=true, to_apply=%add | all-reduce | flops 256 | bytes 2048
  170.8 30.4 %all-gather.10.cloned.1.call-done = f32[256,64,64]{2,1,0:T(8,128)} async-done(((f32[16,64,64]{2,1,0:T(8,128)}), f32[256,64,64]{2,1,0:T(8,128)}) %all-gather.10.cloned.1.call-update) | async-done | bytes 4194320 | tf_op jit(solution)/shard_map/all_gather | solution.py:10
  201.2 18.3 %while.48 = (s32[]{:T(128)}, f32[16]{0:T(128)S(1)}, f32[16,64,64]{2,1,0:T(8,128)S(1)}, s32[]{:T(128)}, f32[16,16]{1,0:T(8,128)S(1)}, /*index=5*/f32[16,16,64,64]{3,2,1,0:T(8,128)}) while((s32[]{:T(128)}, f32[16]{0:T(128)S(1)}, f32[16,64,64]{2,1,0:T(8,128)S(1)}, s32[]{:T(128)}, f32[16,16]{1,0:T(8,128)S(1)}, ...), condition=%wide.region_5.6_spmd.clone.clone, body=%wide.region_4.5_spmd.clone.sunk.clone | while | flops 262196 | bytes 786851 | solution.py:19
  219.5 2.0 add_select_fusion
  221.6 54.5 %all-gather.12.cloned.1.call-done = f32[256,64,64]{2,1,0:T(8,128)} async-done(((f32[16,64,64]{2,1,0:T(8,128)}), f32[256,64,64]{2,1,0:T(8,128)}) %all-gather.12.cloned.1.call-update) | async-done | bytes 4194320 | tf_op jit(solution)/shard_map/all_gather | solution.py:24
  276.1 5.2 %reduce_sum.28 = f32[16,64,64]{2,1,0:T(8,128)} reduce(f32[16,16,64,64]{3,2,1,0:T(8,128)} %bitcast.135, f32[]{:T(128)} %constant.87.clone.1), dimensions={0}, to_apply=%region_7.8 | reduce | flops 983040 | bytes 4456452 | tf_op jit(solution)/shard_map/reduce_sum | solution.py:24
  283.7 23.1 %all-reduce.1 = f32[256]{0:T(256)S(1)} all-reduce(f32[256]{0:T(256)S(1)} %fusion.37), channel_id=4, replica_groups=mesh['outer'=16,'inner'=16] {'inner'}, use_global_device_ids=true, to_apply=%add.1 | all-reduce | flops 256 | bytes 2048
  307.2 34.4 %all-reduce.2 = f32[256]{0:T(256)S(1)} all-reduce(f32[256]{0:T(256)S(1)} %dynamic-update-slice.2), channel_id=5, replica_groups=mesh['outer'=16,'inner'=16] {'outer'}, use_global_device_ids=true, to_apply=%add.2 | all-reduce | flops 256 | bytes 2048
  341.7 14.2 %all-gather.14.cloned.1.call-done = f32[256,64,64]{2,1,0:T(8,128)} async-done(((f32[16,64,64]{2,1,0:T(8,128)}), f32[256,64,64]{2,1,0:T(8,128)}) %all-gather.14.cloned.1.call-update) | async-done | bytes 4194320 | tf_op jit(solution)/shard_map/all_gather | solution.py:10
  355.9 18.2 %while.49 = (s32[]{:T(128)}, f32[16,64,64]{2,1,0:T(8,128)S(1)}, s32[]{:T(128)}, f32[16,16]{1,0:T(8,128)S(1)}, f32[16,16,64,64]{3,2,1,0:T(8,128)}) while((s32[]{:T(128)}, f32[16,64,64]{2,1,0:T(8,128)S(1)}, s32[]{:T(128)}, f32[16,16]{1,0:T(8,128)S(1)}, f32[16,16,64,64]{3,2,1,0:T(8,128)}) %tuple.107), condition=%wide.region_9.10_spmd.clone.clone, body=%wide.region_8.9_spmd.clone.sunk.clone | while | flops 262148 | bytes 786713 | solution.py:19
  374.1 2.9 multiply_reduce_fusion
  379.3 1.9 convolution_convert_fusion
  (285 shorter events, 94.5 us)
Async XLA Ops:
  6.5 1.6 copy-start
  6.5 194.6 %all-gather.10.cloned.1.call-start = ((), (), s32[]{:S(2)}) async-start(), calls=%async_computation | async-start | bytes 8912896 | tf_op jit(solution)/shard_map/all_gather | solution.py:10
  22.6 2.3 copy-start.3
  25.0 115.8 %copy-start.6 = (u32[256]{0:T(256)S(1)}, u32[256]{0:T(256)}, u32[]{:S(2)}) copy-start(u32[256]{0:T(256)} %constant.98) | copy-start | bytes 3076
  140.6 60.5 %copy-start.1 = (bf16[16,384,64]{1,2,0:T(8,128)(2,1)}, bf16[16,384,64]{1,2,0:T(8,128)(2,1)S(1)}, u32[]{:S(2)}) copy-start(bf16[16,384,64]{1,2,0:T(8,128)(2,1)S(1)} %get-tuple-element.595) | copy-start | bytes 2359300
  140.7 135.4 %all-gather.12.cloned.1.call-start = ((), (), s32[]{:S(2)}) async-start(), calls=%async_computation.1 | async-start | bytes 8912896 | tf_op jit(solution)/shard_map/all_gather | solution.py:24
  221.5 134.4 %all-gather.14.cloned.1.call-start = ((), (), s32[]{:S(2)}) async-start(), calls=%async_computation.2 | async-start | bytes 8912896 | tf_op jit(solution)/shard_map/all_gather | solution.py:10
  276.1 5.3 %copy-start.5 = (u32[256]{0:T(256)S(1)}, u32[256]{0:T(256)}, u32[]{:S(2)}) copy-start(u32[256]{0:T(256)} %constant.108) | copy-start | bytes 3076
  377.0 0.7 copy-start.4
  377.7 1.6 copy-start.2
Sparse Core Ops, SparseCore 0:
  140.8 60.3 all-gather.9
  221.6 54.3 all-gather.11
  281.4 74.4 all-gather.13
